TPU v7x, 256 devices: a whole 4x4x8 slice. The times are simulated.
256 devices in a mesh: mp: 4 (over y), nodes: 64 (over z, x, core).
Axes of the slice: x: 4, y: 4, z: 8, core: 2. Of those that a mesh axis runs over, the one named last changes fastest.
Arguments:
- grid_latent: float32 [131072, 512], P('nodes'), may hold values from -6 to 6
- mesh_latent: float32 [8192, 512], P('nodes'), may hold values from -250 to 250
- enc_grid_w: float32 [512, 512], P(None, 'mp'), may hold values from -0.25 to 0.25
- enc_mesh_w: float32 [512, 512], P(None, 'mp'), may hold values from -0.25 to 0.25
- enc_out_w: float32 [512, 512], P('mp'), may hold values from -0.25 to 0.25
- block_gain: float32 [512], replicated, may hold values from 0.5 to 1.5
- query_w: float32 [512, 512], P(None, 'mp'), may hold values from -1 to 1
- key_w: float32 [512, 512], P(None, 'mp'), may hold values from -1 to 1
- value_w: float32 [512, 512], P(None, 'mp'), may hold values from -0.25 to 0.25
- out_w: float32 [512, 512], P('mp'), may hold values from -0.25 to 0.25
- up_w: float32 [512, 2048], P(None, 'mp'), may hold values from -0.25 to 0.25
- down_w: float32 [2048, 512], P('mp'), may hold values from -0.125 to 0.125
- dec_gain: float32 [512], replicated, may hold values from 0.5 to 1.5
- dec_grid_w: float32 [512, 512], P(None, 'mp'), may hold values from -0.25 to 0.25
- dec_mesh_w: float32 [512, 512], P(None, 'mp'), may hold values from -0.25 to 0.25
- dec_out_w: float32 [512, 512], P('mp'), may hold values from -0.25 to 0.25
- neighbor_blocks: int32 [64, 16], replicated, may hold values from 0 to 63, as said below
- enc_tiles: int32 [2048, 2], P('nodes'), may hold values from -1 to 1023, as said below
- enc_edges: int32 [2048, 2, 128], P('nodes'), may hold values from 0 to 127
- dec_tiles: int32 [3072, 2], P('nodes'), may hold values from 0 to 1023, as said below
- dec_edges: int32 [3072, 2, 128], P('nodes'), may hold values from 0 to 127
Outputs:
- grid_out: float32 [131072, 512], P('nodes', 'mp')
Inputs may be any that keep to these rules, and one draw needn't show every extreme that they name: `neighbor_blocks`: rows i * 1 to (i + 1) - 1 are the query blocks of index i of nodes; among all entries of those rows, the blocks of any one index j of nodes (ids j * 1 to (j + 1) - 1) are named at most 1 times, and for every i some j is named exactly 1 times. Entries may repeat. `enc_tiles`: tile slots i * 32 to (i + 1) * 32 - 1 belong to index i of nodes; a live tile names a grid block and a mesh block both of index i; an unused slot holds -1 in both columns; on each index the live slots come first, their number differs between indices, and some index has all 32 slots live. `dec_tiles`: tiles i * 48 to (i + 1) * 48 - 1 belong to index i of nodes; each names a grid block of index i and a mesh block of index i - 1, i or i + 1 of nodes (counted around the axis).
All inputs are finite; a program needn't handle non-finite values.
Results may differ from a plain program's by a relative error of at most 0.000098.
Values sent between devices are 32-bit elements; how exact they have to be, the bound alone decides.
A program may use at most 128 MiB of HBM per device.

v0:
```python
import math
import jax
import jax.numpy as jnp
from jax import lax
from jax.sharding import PartitionSpec as P

HEAD_DIM = 128
NODE_BLOCK = 128
FULL_PRECISION = lax.Precision.HIGHEST


def copy_for_each(shard, axis):
    devices = lax.axis_size(axis)
    return lax.all_to_all(
        jnp.broadcast_to(shard[None], (devices, *shard.shape)), axis, 0, 0, tiled=True
    )


def taken_together(shard, axis):
    everything = copy_for_each(shard, axis)
    return jnp.sum(everything, axis=0)


def padded(shard, sides, width):
    for axis, dim in sides:
        devices, length = (lax.axis_size(axis), shard.shape[dim])
        up = [(i, (i + 1) % devices) for i in range(devices)]
        down = [(j, i) for i, j in up]
        last = lax.slice_in_dim(shard, length - width, length, axis=dim)
        initial = lax.slice_in_dim(shard, 0, width, axis=dim)
        before = lax.ppermute(last, axis, up)
        after = lax.ppermute(initial, axis, down)
        shard = jnp.concatenate([before, shard, after], axis=dim)
    return shard


def product(matrix, weight):
    return jnp.dot(matrix, weight, precision=FULL_PRECISION, preferred_element_type=jnp.float32)


def layer_norm(inputs, scales):
    centre = jnp.mean(inputs, axis=-1, keepdims=True)
    shifted = inputs - centre
    spread = jnp.mean(shifted * shifted, axis=-1, keepdims=True)
    return shifted * lax.rsqrt(spread + 1e-05) * scales


def edge_pass(
    source_side, target_side, source_block, target_block, edge_ids, tile_live, target_blocks
):
    source = source_block[:, None] * NODE_BLOCK + edge_ids[:, 0, :]
    target = target_block[:, None] * NODE_BLOCK + edge_ids[:, 1, :]
    message = jax.nn.silu(source_side[source] + target_side[target]) * tile_live[:, None, None]
    within = (edge_ids[:, 1, :][:, None, :] == jnp.arange(NODE_BLOCK)[None, :, None]).astype(
        jnp.float32
    )
    tile_sums = jnp.einsum("tne,teh->tnh", within, message, precision=FULL_PRECISION)
    placing = (target_block[None, :] == jnp.arange(target_blocks)[:, None]).astype(jnp.float32)
    summed = jnp.einsum("bt,tnh->bnh", placing, tile_sums, precision=FULL_PRECISION)
    return summed.reshape(target_blocks * NODE_BLOCK, -1)


def per_device(
    grid_latent,
    mesh_latent,
    enc_grid_w,
    enc_mesh_w,
    enc_out_w,
    block_gain,
    query_w,
    key_w,
    value_w,
    out_w,
    up_w,
    down_w,
    dec_gain,
    dec_grid_w,
    dec_mesh_w,
    dec_out_w,
    neighbor_blocks,
    enc_tiles,
    enc_edges,
    dec_tiles,
    dec_edges,
):
    me_node = lax.axis_index("nodes")
    nodes_count = lax.axis_size("nodes")
    grid_rows = grid_latent.shape[0]
    node_rows = mesh_latent.shape[0]
    grid_blocks = grid_rows // NODE_BLOCK
    node_blocks = node_rows // NODE_BLOCK
    grid_enc = product(grid_latent, enc_grid_w)
    mesh_enc = product(mesh_latent, enc_mesh_w)
    tile_live = enc_tiles[:, 0] >= 0
    source_block = jnp.where(tile_live, enc_tiles[:, 0] - me_node * grid_blocks, 0)
    target_block = jnp.where(tile_live, enc_tiles[:, 1] - me_node * node_blocks, 0)
    enc_agg = edge_pass(
        grid_enc,
        mesh_enc,
        source_block,
        target_block,
        enc_edges,
        tile_live.astype(jnp.float32),
        node_blocks,
    )
    enc_total = taken_together(product(enc_agg, enc_out_w), "mp")
    mesh_one = mesh_latent + enc_total
    normed = layer_norm(mesh_one, block_gain)
    queries = product(normed, query_w)
    key_rows = product(normed, key_w)
    value_rows = product(normed, value_w)
    head_cols = queries.shape[1]
    heads_here = head_cols // HEAD_DIM
    key_values = jnp.concatenate([key_rows, value_rows], axis=1)
    query_blocks = queries.reshape(node_blocks, NODE_BLOCK, heads_here, HEAD_DIM)
    own_lists = lax.dynamic_slice_in_dim(neighbor_blocks, me_node * node_blocks, node_blocks, 0)
    key_piece = lax.all_gather(key_values, "nodes", axis=0, tiled=True)
    running_max = jnp.full((node_blocks, heads_here, NODE_BLOCK), -1e30, jnp.float32)
    row_count = key_piece.shape[0]
    piece_block = jnp.arange(row_count) // NODE_BLOCK
    repeats = jnp.sum(
        (own_lists[:, :, None] == piece_block[None, None, :]).astype(jnp.float32), axis=1
    )
    near_keys = key_piece[:, :head_cols].reshape(row_count, heads_here, HEAD_DIM)
    near_values = key_piece[:, head_cols:].reshape(row_count, heads_here, HEAD_DIM)
    scores = jnp.einsum(
        "bqhd,khd->bhqk", query_blocks, near_keys, precision=FULL_PRECISION
    ) / math.sqrt(HEAD_DIM)
    scores = jnp.where((repeats > 0)[:, None, None, :], scores, -1e30)
    new_max = jnp.maximum(running_max, jnp.max(scores, axis=-1))
    weights = jnp.exp(scores - new_max[..., None]) * repeats[:, None, None, :]
    running_sum = jnp.sum(weights, axis=-1)
    running_out = jnp.einsum("bhqk,khd->bhqd", weights, near_values, precision=FULL_PRECISION)
    running_max, running_sum, running_out = (new_max, running_sum, running_out)
    attended = (
        (running_out / running_sum[..., None]).transpose(0, 2, 1, 3).reshape(node_rows, head_cols)
    )
    hidden = jax.nn.silu(product(normed, up_w))
    block_total = taken_together(product(attended, out_w) + product(hidden, down_w), "mp")
    mesh_two = mesh_one + block_total
    mesh_normed = layer_norm(mesh_two, dec_gain)
    all_blocks = node_blocks * nodes_count
    dec_source = (dec_tiles[:, 0] - (me_node - 1) * node_blocks) % all_blocks
    dec_target = dec_tiles[:, 1] - me_node * grid_blocks
    mesh_dec = product(mesh_normed, dec_mesh_w)
    grid_dec = product(grid_latent, dec_grid_w)
    beside_all = padded(mesh_dec, (("nodes", 0),), node_rows)
    every_tile = jnp.ones((dec_tiles.shape[0],), jnp.float32)
    dec_agg = edge_pass(
        beside_all, grid_dec, dec_source, dec_target, dec_edges, every_tile, grid_blocks
    )
    decoded = lax.psum_scatter(product(dec_agg, dec_out_w), "mp", scatter_dimension=1, tiled=True)
    share_cols = decoded.shape[1]
    grid_share = lax.dynamic_slice_in_dim(
        grid_latent, lax.axis_index("mp") * share_cols, share_cols, 1
    )
    return grid_share + decoded


def solution(mesh):
    in_specs = (
        P("nodes", None),
        P("nodes", None),
        P(None, "mp"),
        P(None, "mp"),
        P("mp", None),
        P(),
        P(None, "mp"),
        P(None, "mp"),
        P(None, "mp"),
        P("mp", None),
        P(None, "mp"),
        P("mp", None),
        P(),
        P(None, "mp"),
        P(None, "mp"),
        P("mp", None),
        P(),
        P("nodes", None),
        P("nodes", None, None),
        P("nodes", None),
        P("nodes", None, None),
    )
    out_specs = P("nodes", "mp")
    return jax.shard_map(
        per_device, mesh=mesh, in_specs=in_specs, out_specs=out_specs, check_vma=False
    )
```

profile of v0, /device:TPU:1, one launch (start us, length us, event | category | flops | bytes accessed | tf_op | source)
XLA Modules:
  0.0 320.2 jit_solution(5665436345619726725)
XLA Ops:
  8.1 0.9 fusion.91
  8.9 5.2 %fusion.94 = f32[2048,128]{1,0:T(8,128)S(1)} fusion(f32[2048,512]{1,0:T(8,128)} %param.21, f32[512,128]{1,0:T(8,128)} %param.23), kind=kOutput, calls=%fused_computation.123 | convolution fusion | flops 1610612736 | bytes 5505024 | tf_op jit(solution)/shard_map/dot_general | solution.py:38
  14.3 14.1 %gather_fusion = f32[4096,128]{1,0:T(8,128)} fusion(f32[2048,128]{1,0:T(8,128)S(1)} %fusion.94, s32[4096]{0:T(1024)S(1)} %get-tuple-element.20), kind=kCustom, calls=%fused_computation | custom fusion | bytes 4210688 | tf_op jit(solution)/shard_map/gather | solution.py:53
  28.8 14.1 %gather_fusion.1 = f32[4096,128]{1,0:T(8,128)} fusion(f32[128,128]{1,0:T(8,128)S(1)} %fusion.95, s32[4096]{0:T(1024)S(1)} %get-tuple-element.21), kind=kCustom, calls=%fused_computation.1 | custom fusion | bytes 4210688 | tf_op jit(solution)/shard_map/gather | solution.py:53
  42.9 1.8 add.221
  44.7 1.9 fusion.19
  46.6 2.0 fusion.15
  49.1 19.0 %all_to_all.10 = f32[4,128,512]{2,1,0:T(8,128)S(1)} all-to-all(f32[4,128,512]{2,1,0:T(8,128)S(1)} %broadcast_in_dim.17), channel_id=1, replica_groups=mesh['mp'=4,'nodes'=64] {'mp'}, dimensions={0} | all-to-all | bytes 2097152 | tf_op jit(solution)/shard_map/all_to_all | solution.py:14
  68.2 1.1 fusion.89
  69.6 1.6 fusion.87
  71.2 1.6 fusion.86
  73.9 1.4 fusion.85
  76.8 84.9 %all-gather.2.cloned.1.call-done = f32[8192,256]{0,1:T(8,128)} async-done(((f32[128,256]{0,1:T(8,128)}), f32[8192,256]{0,1:T(8,128)}) %all-gather.2.cloned.1.call-update) | async-done | bytes 8388624 | tf_op jit(solution)/shard_map/all_gather | solution.py:117
  161.6 10.2 %fusion.92 = (f32[128]{0:T(128)S(1)}, f32[1,8192,1,128]{3,1,2,0:T(8,128)S(1)}) fusion(f32[128,128]{1,0:T(8,128)S(1)} %fusion.85, f32[8192,256]{0,1:T(8,128)} %all-gather.2.cloned.1.call-done, pred[8192]{0:T(1024)(128)(4,1)S(1)} %broadcast_compare_fusion), kind=kOutput, calls=%fused_computation.121 | convolution fusion | flops 1613758336 | bytes 8462848 | tf_op jit(solution)/shard_map/bqhd,khd->bhqk/dot_general | solution.py:126
  171.8 3.5 %fusion.6 = f32[128]{0:T(128)S(1)} fusion(f32[1,8192,1,128]{3,1,2,0:T(8,128)S(1)} %get-tuple-element.19, f32[8192]{0:T(1024)S(1)} %convert_reduce_fusion, f32[128]{0:T(128)S(1)} %broadcast_maximum_fusion), kind=kLoop, calls=%fused_computation.12 | loop fusion | flops 3145600 | bytes 4228096 | tf_op jit(solution)/shard_map/reduce_sum | solution.py:132
  175.3 5.0 %fusion.38 = f32[128,128]{0,1:T(8,128)S(1)} fusion(f32[1,8192,1,128]{3,1,2,0:T(8,128)S(1)} %get-tuple-element.19, f32[8192]{0:T(1024)S(1)} %convert_reduce_fusion, f32[128]{0:T(128)S(1)} %broadcast_maximum_fusion, f32[8192,256]{0,1:T(8,128)S(1)} %copy-done.1, f32[128]{0:T(128)S(1)} %fusion.6), kind=kOutput, calls=%fused_computation.39 | convolution fusion | flops 1612726272 | bytes 8487936 | tf_op jit(solution)/shard_map/bhqk,khd->bhqd/dot_general | solution.py:133
  180.8 1.1 broadcast_in_dim.21
  181.9 4.0 %all-to-all-start.1 = ((f32[4,128,512]{2,1,0:T(8,128)}), f32[4,128,512]{2,1,0:T(8,128)S(1)}, u32[]{:S(2)}, u32[]{:S(2)}) async-start(f32[4,128,512]{2,1,0:T(8,128)} %broadcast_in_dim.21), calls=%async_computation.1 | async-start | bytes 2097152 | tf_op jit(solution)/shard_map/all_to_all | solution.py:14
  186.0 5.2 %fusion.97 = f32[2048,128]{1,0:T(8,128)S(1)} fusion(f32[2048,512]{1,0:T(8,128)} %param.21, f32[512,128]{1,0:T(8,128)} %param.34), kind=kOutput, calls=%fused_computation.126 | convolution fusion | flops 1610612736 | bytes 5505024 | tf_op jit(solution)/shard_map/dot_general | solution.py:38
  191.2 9.3 %all-to-all-done.1 = f32[4,128,512]{2,1,0:T(8,128)S(1)} async-done(((f32[4,128,512]{2,1,0:T(8,128)}), f32[4,128,512]{2,1,0:T(8,128)S(1)}, u32[]{:S(2)}, u32[]{:S(2)}) %all-to-all-start.1) | async-done | bytes 1048608 | tf_op jit(solution)/shard_map/all_to_all | solution.py:14
  200.6 0.8 reduce_sum.77
  201.4 1.1 fusion.88
  202.6 1.4 fusion.46
  204.0 3.1 collective-permute-start
  207.2 20.9 %gather_fusion.3 = f32[6144,128]{1,0:T(8,128)} fusion(f32[2048,128]{1,0:T(8,128)S(1)} %fusion.97, s32[6144]{0:T(1024)S(1)} %get-tuple-element.23), kind=kCustom, calls=%fused_computation.3 | custom fusion | bytes 6316032 | tf_op jit(solution)/shard_map/gather | solution.py:53
  228.1 20.9 %gather_fusion.2 = f32[6144,128]{1,0:T(8,128)} fusion(f32[384,128]{1,0:T(8,128)S(1)} %pad_maximum_fusion, s32[6144]{0:T(1024)S(1)} %get-tuple-element.22), kind=kCustom, calls=%fused_computation.2 | custom fusion | bytes 6316032 | tf_op jit(solution)/shard_map/gather | solution.py:53
  249.1 3.2 add.222
  252.2 2.9 fusion.9
  255.2 2.9 fusion.7
  258.5 4.9 %fusion.98 = f32[2048,512]{1,0:T(8,128)} fusion(f32[2048,128]{1,0:T(8,128)S(1)} %bitcast.97, f32[128,512]{1,0:T(8,128)S(1)} %copy-done.8), kind=kOutput, calls=%fused_computation.127 | convolution fusion | flops 1610612736 | bytes 5505024 | tf_op jit(solution)/shard_map/dot_general | solution.py:38
  263.4 47.3 %reduce-scatter.2.cloned.1.call-done = f32[2048,128]{1,0:T(8,128)} async-done(((f32[2048,512]{1,0:T(8,128)}), f32[2048,128]{1,0:T(8,128)}) %reduce-scatter.2.cloned.1.call-update) | async-done | bytes 1048592 | tf_op jit(solution)/shard_map/reduce_scatter | solution.py:152
  310.7 2.6 dynamic-slice_add_fusion
  (64 shorter events, 6.5 us)
Async XLA Ops:
  6.5 68.7 %copy-start = (f32[512,512]{1,0:T(8,128)S(1)}, f32[512,512]{1,0:T(8,128)}, u32[]{:S(2)}) copy-start(f32[512,512]{1,0:T(8,128)} %param.31) | copy-start | bytes 3145732
  6.5 155.1 %all-gather.2.cloned.1.call-start = ((), (), s32[]{:S(2)}) async-start(), calls=%async_computation.3 | async-start | bytes 8519680 | tf_op jit(solution)/shard_map/all_gather | solution.py:117
  14.2 14.1 %copy-start.4 = (f32[128,512]{1,0:T(8,128)S(1)}, f32[128,512]{1,0:T(8,128)}, u32[]{:S(2)}) copy-start(f32[128,512]{1,0:T(8,128)} %param.22) | copy-start | bytes 786436
  14.3 14.1 %copy-start.5 = (f32[512,128]{1,0:T(8,128)S(1)}, f32[512,128]{1,0:T(8,128)}, u32[]{:S(2)}) copy-start(f32[512,128]{1,0:T(8,128)} %param.24) | copy-start | bytes 786436
  28.8 14.1 %copy-start.2 = (f32[4096,128]{1,0:T(8,128)S(1)}, f32[4096,128]{1,0:T(8,128)}, u32[]{:S(2)}) copy-start(f32[4096,128]{1,0:T(8,128)} %gather_fusion) | copy-start | bytes 6291460
  44.7 1.9 copy-start.12
  44.7 3.9 %copy-start.6 = (f32[128,512]{1,0:T(8,128)S(1)}, f32[128,512]{1,0:T(8,128)}, u32[]{:S(2)}) copy-start(f32[128,512]{1,0:T(8,128)} %param.25) | copy-start | bytes 786436
  48.6 21.0 %copy-start.10 = (f32[512]{0:T(512)S(1)}, f32[512]{0:T(512)}, u32[]{:S(2)}) copy-start(f32[512]{0:T(512)} %param.26) | copy-start | bytes 6148
  49.1 24.4 %copy-start.11 = (s32[64,16]{0,1:T(8,128)S(1)}, s32[64,16]{0,1:T(8,128)}, u32[]{:S(2)}) copy-start(s32[64,16]{0,1:T(8,128)} %param.37) | copy-start | bytes 12292
  68.1 7.9 %copy-start.3 = (f32[512,512]{1,0:T(8,128)S(1)}, f32[512,512]{1,0:T(8,128)}, u32[]{:S(2)}) copy-start(f32[512,512]{1,0:T(8,128)} %param.32) | copy-start | bytes 3145732
  161.6 13.7 %copy-start.1 = (f32[8192,256]{0,1:T(8,128)S(1)}, f32[8192,256]{0,1:T(8,128)}, u32[]{:S(2)}) copy-start(f32[8192,256]{0,1:T(8,128)} %all-gather.2.cloned.1.call-done) | copy-start | bytes 25165828
  175.3 5.0 %copy-start.7 = (f32[128,512]{1,0:T(8,128)S(1)}, f32[128,512]{1,0:T(8,128)}, u32[]{:S(2)}) copy-start(f32[128,512]{1,0:T(8,128)} %param.30) | copy-start | bytes 786436
  180.3 5.6 %copy-start.14 = (s32[48,2]{0,1:T(2,128)S(1)}, s32[48,2]{0,1:T(2,128)}, u32[]{:S(2)}) copy-start(s32[48,2]{0,1:T(2,128)} %param.40) | copy-start | bytes 1156
  180.4 5.6 %copy-start.9 = (s32[48,2,128]{2,1,0:T(2,128)S(1)}, s32[48,2,128]{2,1,0:T(2,128)}, u32[]{:S(2)}) copy-start(s32[48,2,128]{2,1,0:T(2,128)} %param.41) | copy-start | bytes 147460
  181.9 18.7 %all-to-all-start.1 = ((f32[4,128,512]{2,1,0:T(8,128)}), f32[4,128,512]{2,1,0:T(8,128)S(1)}, u32[]{:S(2)}, u32[]{:S(2)}) async-start(f32[4,128,512]{2,1,0:T(8,128)} %broadcast_in_dim.21), calls=%async_computation.1 | async-start | bytes 2097152 | tf_op jit(solution)/shard_map/all_to_all | solution.py:14
  185.9 124.8 %reduce-scatter.2.cloned.1.call-start = ((), (), s32[]{:S(2)}) async-start(), calls=%async_computation.4 | async-start | bytes 5242880 | tf_op jit(solution)/shard_map/reduce_scatter | solution.py:152
  186.0 16.6 %copy-start.13 = (f32[512]{0:T(512)S(1)}, f32[512]{0:T(512)}, u32[]{:S(2)}) copy-start(f32[512]{0:T(512)} %param.33) | copy-start | bytes 6148
  204.0 24.1 %collective-permute-start = (f32[128,128]{1,0:T(8,128)S(1)}, f32[128,128]{1,0:T(8,128)S(1)}, u32[]{:S(2)}, u32[]{:S(2)}) collective-permute-start(f32[128,128]{1,0:T(8,128)S(1)} %fusion.46), channel_id=1, source_target_pairs={{0,1},{1,2},{2,3},{3,4},{4,5},{5,6},{6,7},{7,8},{8,9},{9,10},{10,1... | collective-permute-start | bytes 196616 | tf_op jit(solution)/shard_map/ppermute | solution.py:31
  207.1 21.0 %collective-permute-start.1 = (f32[128,128]{1,0:T(8,128)S(1)}, f32[128,128]{1,0:T(8,128)S(1)}, u32[]{:S(2)}, u32[]{:S(2)}) collective-permute-start(f32[128,128]{1,0:T(8,128)S(1)} %fusion.46), channel_id=1, source_target_pairs={{1,0},{2,1},{3,2},{4,3},{5,4},{6,5},{7,6},{8,7},{9,8},{10,9},{11,1... | collective-permute-start | bytes 196616 | tf_op jit(solution)/shard_map/ppermute | solution.py:32
  255.2 3.3 %copy-start.8 = (f32[128,512]{1,0:T(8,128)S(1)}, f32[128,512]{1,0:T(8,128)}, u32[]{:S(2)}) copy-start(f32[128,512]{1,0:T(8,128)} %param.36) | copy-start | bytes 786436
Sparse Core Ops, SparseCore 0:
  73.6 87.9 all-gather.1
  263.6 47.1 reduce-scatter.1
where the time goes:
time: 321 us; the launch traced here: 320 us
  waiting for transfers between devices  142 us (44%)
  local copies, waits for them, and re-layouts  72.8 us (23%)
  matrix products  48.9 us (15%)
  blocking collectives  19 us (6%)
  other arithmetic  17.1 us (5%)
  between operations  13.8 us (4%)
  starting transfers between devices  7.08 us (2%)
    all_gather x1, waiting for transfers between devices, per_device(): key_piece = lax.all_gather(key_values, 'nodes', axis=0, tiled=True)  84.9 us
    reduce_scatter x1, waiting for transfers between devices, per_device(): lax.psum_scatter(product(dec_agg, dec_out_w), 'mp', scatter_dimension=1,...  47.3 us
    gather x2, local copies, waits for them, and re-layouts, edge_pass(): source_side[source] + target_side[target]  35 us
    gather x2, local copies, waits for them, and re-layouts, edge_pass(): target_side[target]  35 us
    dot_general x12, matrix products, product(): jnp.dot(matrix, weight, precision=FULL_PRECISION, preferred_element_type=...  24 us
    all_to_all x1, blocking collectives, copy_for_each(): lax.all_to_all(jnp.broadcast_to(shard[None], (devices, *shard.shape)), ax...  19 us
    dot_general x1, matrix products, per_device(): jnp.einsum('bqhd,khd->bhqk', query_blocks, near_keys, precision=FULL_PREC...  10.2 us
    all_to_all x1, waiting for transfers between devices, copy_for_each(): lax.all_to_all(jnp.broadcast_to(shard[None], (devices, *shard.shape)), ax...  9.34 us
  transfers between devices with their start and end apart: 5, of which 3 were waited for; matrix products, arithmetic and copies ran while one was open for 9% of the time, Pallas kernels for 0%

commit v1 on v0

--- a/solution.py
+++ b/solution.py
@@ -114,7 +114,9 @@
     key_values = jnp.concatenate([key_rows, value_rows], axis=1)
     query_blocks = queries.reshape(node_blocks, NODE_BLOCK, heads_here, HEAD_DIM)
     own_lists = lax.dynamic_slice_in_dim(neighbor_blocks, me_node * node_blocks, node_blocks, 0)
-    key_piece = lax.all_gather(key_values, "nodes", axis=0, tiled=True)
+    key_piece = jnp.concatenate(
+        lax.all_to_all(jnp.stack([key_values] * lax.axis_size("nodes")), "nodes", 0, 0), axis=0
+    )
     running_max = jnp.full((node_blocks, heads_here, NODE_BLOCK), -1e30, jnp.float32)
     row_count = key_piece.shape[0]
     piece_block = jnp.arange(row_count) // NODE_BLOCK

time: 321 us -> 430 us (1.34)
  waiting for transfers between devices: 142 us -> 232 us
  starting transfers between devices: 7.08 us -> 25.3 us
  local copies, waits for them, and re-layouts: 72.8 us -> 77.2 us
    all_to_all x0 -> x1, waiting for transfers between devices: none -> 180 us  [per_device(): lax.all_to_all(jnp.stack([key_values] * lax.axis_size('nodes')), 'nodes',...]
    all_gather x1 -> x0, waiting for transfers between devices: 84.9 us -> none  [per_device(): key_piece = lax.all_gather(key_values, 'nodes', axis=0, tiled=True)]
    all_to_all x0 -> x1, starting transfers between devices: none -> 13.7 us  [per_device(): lax.all_to_all(jnp.stack([key_values] * lax.axis_size('nodes')), 'nodes',...]
    dot_general x1, matrix products: 5 us -> 10.1 us  [per_device(): jnp.einsum('bhqk,khd->bhqd', weights, near_values, precision=FULL_PRECISION)]
    ppermute x1, starting transfers between devices: 3.07 us -> 8.05 us  [padded(): before = lax.ppermute(last, axis, up)]
  transfers between devices with their start and end apart: 5 -> 5, of which waited for: 3 -> 3; matrix products, arithmetic and copies ran while one was open for 9% -> 7% of each run, Pallas kernels for 0% -> 0%
where the time goes in v1:
time: 430 us; the launch traced here: 429 us
  waiting for transfers between devices  232 us (54%)
  local copies, waits for them, and re-layouts  77.2 us (18%)
  matrix products  47.4 us (11%)
  starting transfers between devices  25.3 us (6%)
  blocking collectives  19 us (4%)
  between operations  13.9 us (3%)
  other arithmetic  13.8 us (3%)
    all_to_all x1, waiting for transfers between devices, per_device(): lax.all_to_all(jnp.stack([key_values] * lax.axis_size('nodes')), 'nodes',...  180 us
    reduce_scatter x1, waiting for transfers between devices, per_device(): lax.psum_scatter(product(dec_agg, dec_out_w), 'mp', scatter_dimension=1,...  47.1 us
    gather x2, local copies, waits for them, and re-layouts, edge_pass(): source_side[source] + target_side[target]  35.1 us
    gather x2, local copies, waits for them, and re-layouts, edge_pass(): target_side[target]  35 us
    dot_general x12, matrix products, product(): jnp.dot(matrix, weight, precision=FULL_PRECISION, preferred_element_type=...  20.2 us
    all_to_all x1, blocking collectives, copy_for_each(): lax.all_to_all(jnp.broadcast_to(shard[None], (devices, *shard.shape)), ax...  19 us
    all_to_all x1, starting transfers between devices, per_device(): lax.all_to_all(jnp.stack([key_values] * lax.axis_size('nodes')), 'nodes',...  13.7 us
    dot_general x1, matrix products, per_device(): jnp.einsum('bhqk,khd->bhqd', weights, near_values, precision=FULL_PRECISION)  10.1 us
  transfers between devices with their start and end apart: 5, of which 3 were waited for; matrix products, arithmetic and copies ran while one was open for 7% of the time, Pallas kernels for 0%

profile of v1, /device:TPU:1, one launch (start us, length us, event | category | flops | bytes accessed | tf_op | source)
XLA Modules:
  0.0 429.0 jit_solution(13545191016786041624)
XLA Ops:
  6.5 0.8 convert_bitcast_fusion
  7.3 0.8 multiply_bitcast_fusion.1
  8.1 0.9 fusion.91
  8.9 5.2 %fusion.94 = f32[2048,128]{1,0:T(8,128)S(1)} fusion(f32[2048,512]{1,0:T(8,128)} %param.21, f32[512,128]{1,0:T(8,128)} %param.23), kind=kOutput, calls=%fused_computation.123 | convolution fusion | flops 1610612736 | bytes 5505024 | tf_op jit(solution)/shard_map/dot_general | solution.py:38
  14.3 14.1 %gather_fusion = f32[4096,128]{1,0:T(8,128)} fusion(f32[2048,128]{1,0:T(8,128)S(1)} %fusion.94, s32[4096]{0:T(1024)S(1)} %get-tuple-element.20), kind=kCustom, calls=%fused_computation | custom fusion | bytes 4210688 | tf_op jit(solution)/shard_map/gather | solution.py:53
  28.8 14.1 %gather_fusion.1 = f32[4096,128]{1,0:T(8,128)} fusion(f32[128,128]{1,0:T(8,128)S(1)} %fusion.95, s32[4096]{0:T(1024)S(1)} %get-tuple-element.21), kind=kCustom, calls=%fused_computation.1 | custom fusion | bytes 4210688 | tf_op jit(solution)/shard_map/gather | solution.py:53
  42.9 1.8 add.221
  44.7 1.9 fusion.19
  46.7 2.0 fusion.15
  49.2 19.0 %all_to_all.15 = f32[4,128,512]{2,1,0:T(8,128)S(1)} all-to-all(f32[4,128,512]{2,1,0:T(8,128)S(1)} %broadcast_in_dim.17), channel_id=1, replica_groups=mesh['mp'=4,'nodes'=64] {'mp'}, dimensions={0} | all-to-all | bytes 2097152 | tf_op jit(solution)/shard_map/all_to_all | solution.py:14
  68.6 0.7 fusion.87
  70.0 4.2 stack.2
  74.3 13.7 %all-to-all-start.1 = ((f32[64,128,256]{2,1,0:T(8,128)}), f32[64,128,256]{2,1,0:T(8,128)}, u32[]{:S(2)}, u32[]{:S(2)}) async-start(f32[64,128,256]{2,1,0:T(8,128)} %stack.2), calls=%async_computation.1 | async-start | bytes 16777216 | tf_op jit(solution)/shard_map/all_to_all | solution.py:118
  88.8 0.7 fusion.84
  89.6 0.8 fusion.49
  90.3 180.1 %all-to-all-done.1 = f32[64,128,256]{2,1,0:T(8,128)} async-done(((f32[64,128,256]{2,1,0:T(8,128)}), f32[64,128,256]{2,1,0:T(8,128)}, u32[]{:S(2)}, u32[]{:S(2)}) %all-to-all-start.1) | async-done | bytes 8388640 | tf_op jit(solution)/shard_map/all_to_all | solution.py:118
  270.4 7.3 %fusion.92 = (f32[128]{0:T(128)S(1)}, f32[1,8192,1,128]{3,1,2,0:T(8,128)S(1)}) fusion(f32[128,128]{1,0:T(8,128)S(1)} %fusion.85, f32[8192,256]{1,0:T(8,128)} %bitcast.16, pred[8192]{0:T(1024)(128)(4,1)S(1)} %broadcast_compare_fusion), kind=kOutput, calls=%fused_computation.121 | convolution fusion | flops 1613758336 | bytes 8462848 | tf_op jit(solution)/shard_map/bqhd,khd->bhqk/dot_general | solution.py:128
  277.7 3.5 fusion.6
  281.2 10.1 %fusion.38 = f32[128,128]{0,1:T(8,128)S(1)} fusion(f32[1,8192,1,128]{3,1,2,0:T(8,128)S(1)} %get-tuple-element.19, f32[8192]{0:T(1024)S(1)} %convert_reduce_fusion, f32[128]{0:T(128)S(1)} %broadcast_maximum_fusion, f32[8192,256]{1,0:T(8,128)} %bitcast.16, f32[128]{0:T(128)S(1)} %fusion.6), kind=kOutput, calls=%fused_computation.39 | convolution fusion | flops 1612726272 | bytes 8487936 | tf_op jit(solution)/shard_map/bhqk,khd->bhqd/dot_general | solution.py:135
  291.9 1.1 broadcast_in_dim.21
  293.0 3.5 all-to-all-start.2
  296.6 5.2 %fusion.97 = f32[2048,128]{1,0:T(8,128)S(1)} fusion(f32[2048,512]{1,0:T(8,128)} %param.21, f32[512,128]{1,0:T(8,128)S(1)} %copy-done.12), kind=kOutput, calls=%fused_computation.126 | convolution fusion | flops 1610612736 | bytes 5505024 | tf_op jit(solution)/shard_map/dot_general | solution.py:38
  301.9 5.3 %all-to-all-done.2 = f32[4,128,512]{2,1,0:T(8,128)S(1)} async-done(((f32[4,128,512]{2,1,0:T(8,128)}), f32[4,128,512]{2,1,0:T(8,128)S(1)}, u32[]{:S(2)}, u32[]{:S(2)}) %all-to-all-start.2) | async-done | bytes 1048608 | tf_op jit(solution)/shard_map/all_to_all | solution.py:14
  308.0 8.1 %collective-permute-start = (f32[128,128]{1,0:T(8,128)S(1)}, f32[128,128]{1,0:T(8,128)S(1)}, u32[]{:S(2)}, u32[]{:S(2)}) collective-permute-start(f32[128,128]{1,0:T(8,128)S(1)} %fusion.46), channel_id=1, source_target_pairs={{0,1},{1,2},{2,3},{3,4},{4,5},{5,6},{6,7},{7,8},{8,9},{9,10},{10,1... | collective-permute-start | bytes 196616 | tf_op jit(solution)/shard_map/ppermute | solution.py:31
  316.2 20.9 %gather_fusion.3 = f32[6144,128]{1,0:T(8,128)} fusion(f32[2048,128]{1,0:T(8,128)S(1)} %fusion.97, s32[6144]{0:T(1024)S(1)} %get-tuple-element.23), kind=kCustom, calls=%fused_computation.3 | custom fusion | bytes 6316032 | tf_op jit(solution)/shard_map/gather | solution.py:53
  337.1 21.0 %gather_fusion.2 = f32[6144,128]{1,0:T(8,128)} fusion(f32[384,128]{1,0:T(8,128)S(1)} %pad_maximum_fusion, s32[6144]{0:T(1024)S(1)} %get-tuple-element.22), kind=kCustom, calls=%fused_computation.2 | custom fusion | bytes 6316032 | tf_op jit(solution)/shard_map/gather | solution.py:53
  358.1 3.2 add.222
  361.3 3.0 fusion.9
  364.2 2.9 fusion.7
  367.5 4.9 %fusion.98 = f32[2048,512]{1,0:T(8,128)} fusion(f32[2048,128]{1,0:T(8,128)S(1)} %bitcast.98, f32[128,512]{1,0:T(8,128)S(1)} %copy-done.13), kind=kOutput, calls=%fused_computation.127 | convolution fusion | flops 1610612736 | bytes 5505024 | tf_op jit(solution)/shard_map/dot_general | solution.py:38
  372.4 47.1 %reduce-scatter.2.cloned.1.call-done = f32[2048,128]{1,0:T(8,128)} async-done(((f32[2048,512]{1,0:T(8,128)}), f32[2048,128]{1,0:T(8,128)}) %reduce-scatter.2.cloned.1.call-update) | async-done | bytes 1048592 | tf_op jit(solution)/shard_map/reduce_scatter | solution.py:154
  419.5 2.6 dynamic-slice_add_fusion
  (75 shorter events, 4.8 us)
Async XLA Ops:
  6.5 82.3 %copy-start = (f32[512,512]{1,0:T(8,128)S(1)}, f32[512,512]{1,0:T(8,128)}, u32[]{:S(2)}) copy-start(f32[512,512]{1,0:T(8,128)} %param.31) | copy-start | bytes 3145732
  14.3 14.1 %copy-start.4 = (f32[128,512]{1,0:T(8,128)S(1)}, f32[128,512]{1,0:T(8,128)}, u32[]{:S(2)}) copy-start(f32[128,512]{1,0:T(8,128)} %param.22) | copy-start | bytes 786436
  14.3 14.1 %copy-start.5 = (f32[512,128]{1,0:T(8,128)S(1)}, f32[512,128]{1,0:T(8,128)}, u32[]{:S(2)}) copy-start(f32[512,128]{1,0:T(8,128)} %param.24) | copy-start | bytes 786436
  28.8 14.1 %copy-start.2 = (f32[4096,128]{1,0:T(8,128)S(1)}, f32[4096,128]{1,0:T(8,128)}, u32[]{:S(2)}) copy-start(f32[4096,128]{1,0:T(8,128)} %gather_fusion) | copy-start | bytes 6291460
  44.7 1.9 copy-start.17
  44.7 3.9 copy-start.6
  48.6 19.9 %copy-start.7 = (f32[512,128]{1,0:T(8,128)S(1)}, f32[512,128]{1,0:T(8,128)}, u32[]{:S(2)}) copy-start(f32[512,128]{1,0:T(8,128)} %param.28) | copy-start | bytes 786436
  48.7 19.9 %copy-start.15 = (f32[512]{0:T(512)S(1)}, f32[512]{0:T(512)}, u32[]{:S(2)}) copy-start(f32[512]{0:T(512)} %param.26) | copy-start | bytes 6148
  49.0 20.2 %copy-start.8 = (f32[512,128]{1,0:T(8,128)S(1)}, f32[512,128]{1,0:T(8,128)}, u32[]{:S(2)}) copy-start(f32[512,128]{1,0:T(8,128)} %param.29) | copy-start | bytes 786436
  74.3 13.7 %copy-start.16 = (s32[64,16]{0,1:T(8,128)S(1)}, s32[64,16]{0,1:T(8,128)}, u32[]{:S(2)}) copy-start(s32[64,16]{0,1:T(8,128)} %param.37) | copy-start | bytes 12292
  74.3 14.1 %copy-start.9 = (f32[512,128]{1,0:T(8,128)S(1)}, f32[512,128]{1,0:T(8,128)}, u32[]{:S(2)}) copy-start(f32[512,128]{1,0:T(8,128)} %param.27) | copy-start | bytes 786436
  74.3 15.3 %copy-start.3 = (f32[512,512]{1,0:T(8,128)S(1)}, f32[512,512]{1,0:T(8,128)}, u32[]{:S(2)}) copy-start(f32[512,512]{1,0:T(8,128)} %param.32) | copy-start | bytes 3145732
  74.3 196.1 %all-to-all-start.1 = ((f32[64,128,256]{2,1,0:T(8,128)}), f32[64,128,256]{2,1,0:T(8,128)}, u32[]{:S(2)}, u32[]{:S(2)}) async-start(f32[64,128,256]{2,1,0:T(8,128)} %stack.2), calls=%async_computation.1 | async-start | bytes 16777216 | tf_op jit(solution)/shard_map/all_to_all | solution.py:118
  281.2 10.2 %copy-start.10 = (f32[128,512]{1,0:T(8,128)S(1)}, f32[128,512]{1,0:T(8,128)}, u32[]{:S(2)}) copy-start(f32[128,512]{1,0:T(8,128)} %param.30) | copy-start | bytes 786436
  291.4 5.1 %copy-start.19 = (s32[48,2]{0,1:T(2,128)S(1)}, s32[48,2]{0,1:T(2,128)}, u32[]{:S(2)}) copy-start(s32[48,2]{0,1:T(2,128)} %param.40) | copy-start | bytes 1156
  291.4 5.2 %copy-start.14 = (s32[48,2,128]{2,1,0:T(2,128)S(1)}, s32[48,2,128]{2,1,0:T(2,128)}, u32[]{:S(2)}) copy-start(s32[48,2,128]{2,1,0:T(2,128)} %param.41) | copy-start | bytes 147460
  291.4 5.2 %copy-start.12 = (f32[512,128]{1,0:T(8,128)S(1)}, f32[512,128]{1,0:T(8,128)}, u32[]{:S(2)}) copy-start(f32[512,128]{1,0:T(8,128)} %param.34) | copy-start | bytes 786436
  293.0 14.2 %all-to-all-start.2 = ((f32[4,128,512]{2,1,0:T(8,128)}), f32[4,128,512]{2,1,0:T(8,128)S(1)}, u32[]{:S(2)}, u32[]{:S(2)}) async-start(f32[4,128,512]{2,1,0:T(8,128)} %broadcast_in_dim.21), calls=%async_computation.2 | async-start | bytes 2097152 | tf_op jit(solution)/shard_map/all_to_all | solution.py:14
  296.5 123.0 %reduce-scatter.2.cloned.1.call-start = ((), (), s32[]{:S(2)}) async-start(), calls=%async_computation.4 | async-start | bytes 5242880 | tf_op jit(solution)/shard_map/reduce_scatter | solution.py:154
  296.6 11.0 %copy-start.11 = (f32[512,128]{1,0:T(8,128)S(1)}, f32[512,128]{1,0:T(8,128)}, u32[]{:S(2)}) copy-start(f32[512,128]{1,0:T(8,128)} %param.35) | copy-start | bytes 786436
  296.6 11.0 %copy-start.18 = (f32[512]{0:T(512)S(1)}, f32[512]{0:T(512)}, u32[]{:S(2)}) copy-start(f32[512]{0:T(512)} %param.33) | copy-start | bytes 6148
  308.0 29.1 %collective-permute-start = (f32[128,128]{1,0:T(8,128)S(1)}, f32[128,128]{1,0:T(8,128)S(1)}, u32[]{:S(2)}, u32[]{:S(2)}) collective-permute-start(f32[128,128]{1,0:T(8,128)S(1)} %fusion.46), channel_id=1, source_target_pairs={{0,1},{1,2},{2,3},{3,4},{4,5},{5,6},{6,7},{7,8},{8,9},{9,10},{10,1... | collective-permute-start | bytes 196616 | tf_op jit(solution)/shard_map/ppermute | solution.py:31
  316.1 21.0 %collective-permute-start.1 = (f32[128,128]{1,0:T(8,128)S(1)}, f32[128,128]{1,0:T(8,128)S(1)}, u32[]{:S(2)}, u32[]{:S(2)}) collective-permute-start(f32[128,128]{1,0:T(8,128)S(1)} %fusion.46), channel_id=1, source_target_pairs={{1,0},{2,1},{3,2},{4,3},{5,4},{6,5},{7,6},{8,7},{9,8},{10,9},{11,1... | collective-permute-start | bytes 196616 | tf_op jit(solution)/shard_map/ppermute | solution.py:32
  364.2 3.3 copy-start.13
  372.4 49.7 %copy-start.1 = (f32[512,512]{1,0:T(8,128)S(1)}, f32[512,512]{1,0:T(8,128)}, u32[]{:S(2)}) copy-start(f32[512,512]{1,0:T(8,128)} %param.31) | copy-start | bytes 3145732
Sparse Core Ops, SparseCore 0:
  372.6 46.9 reduce-scatter.1
